TPU v7x, 256 devices: a whole 4x4x8 slice. The times are simulated.
256 devices in a mesh: dom: 16 (over z, y_lo), grp: 16 (over y_hi, x, core).
Axes of the slice: x: 4, y: 4 (y_hi: 2, y_lo: 2; y = y_hi * 2 + y_lo), z: 8, core: 2. Of those that a mesh axis runs over, the one named last changes fastest.
Arguments:
- psi: float32 [1024, 32768], P('grp', 'dom'), may hold values from -0.078125 to 0.078125
- proj: float32 [16, 128, 2048], P('dom'), may hold values from -6 to 6
- offsets: int32 [16], P('dom'), may hold values from 0 to 112
- species: int32 [128], replicated, may hold values from 0 to 3
- augment_q: float32 [4, 8, 8], replicated, as said below
- rotation: float32 [1024, 1024], replicated, may hold values from -0.1875 to 0.1875
- occupation: float32 [1024], replicated, may hold values from 0.1 to 1
Outputs:
- new_psi: float32 [1024, 32768], P('grp', 'dom')
- density: float32 [32768], P(('dom', 'grp'))
- rho_ij: float32 [128, 64], replicated
Inputs may be any that keep to these rules, and one draw needn't show every extreme that they name: augment_q[s] is symmetric with a positive diagonal that dominates each row.
All inputs are finite; a program needn't handle non-finite values.
Results may differ from a plain program's by a relative error of at most 0.0003.
Values sent between devices are 32-bit elements; how exact they have to be, the bound alone decides.
A program may use at most 128 MiB of HBM per device.

v0:
```python
import jax
import jax.numpy as jnp
from jax import lax
from jax.sharding import PartitionSpec as P

highest = lax.Precision.HIGHEST


def product(left, right):
    return jnp.dot(left, right, precision=highest, preferred_element_type=jnp.float32)


def on_device(psi, proj, offsets, species, augment_q, rotation, occupation):
    local_states, cells = psi.shape
    groups = lax.axis_size("grp")
    all_states = local_states * groups
    total_cells = cells * lax.axis_size("dom")
    atoms = species.shape[0]
    kinds = augment_q.shape[0]
    channels = augment_q.shape[1]
    columns = atoms * channels
    partial_value = product(psi, proj[0].T)
    placed = lax.dynamic_update_slice(
        jnp.zeros((local_states, columns), jnp.float32),
        partial_value,
        (jnp.int32(0), offsets[0] * channels),
    )
    coeff = lax.psum(placed, "dom")
    table = (species[:, None] == jnp.arange(kinds, dtype=jnp.int32)[None, :]).astype(jnp.float32)
    per_atom = jnp.einsum("as,sij->aij", table, augment_q, precision=highest)
    weighted = jnp.einsum(
        "nai,aij->naj", coeff.reshape(local_states, atoms, channels), per_atom, precision=highest
    ).reshape(local_states, columns)
    pieces = (
        lax.all_gather(psi, "grp", axis=0, tiled=True),
        lax.all_gather(coeff, "grp", axis=0, tiled=True),
    )
    grid_part = product(psi, pieces[0].T)
    paw_part = product(weighted, pieces[1].T)
    gram_rows_own = lax.psum(grid_part, "dom") + paw_part
    gram = lax.all_gather(gram_rows_own, "grp", axis=0, tiled=True)
    lower = jnp.linalg.cholesky(gram)
    mixing = lax.linalg.triangular_solve(
        lower, rotation, left_side=True, lower=True, transpose_a=True
    )
    first = lax.axis_index("grp") * local_states
    own_columns = lax.dynamic_slice_in_dim(mixing, first, local_states, 1)
    pieces = (
        lax.all_gather(psi, "grp", axis=0, tiled=True),
        lax.all_gather(coeff, "grp", axis=0, tiled=True),
    )
    new_psi = product(own_columns.T, pieces[0])
    new_coeff = product(own_columns.T, pieces[1])
    own_occupation = lax.dynamic_slice_in_dim(occupation, first, local_states, 0)
    weight = own_occupation / all_states
    local_density = jnp.sum(weight[:, None] * new_psi * new_psi, axis=0) * total_cells
    shaped = new_coeff.reshape(local_states, atoms, channels)
    local_channels = jnp.einsum(
        "n,nai,naj->aij", own_occupation, shaped, shaped, precision=highest
    ).reshape(atoms, channels * channels)
    density = lax.psum_scatter(local_density, "grp", scatter_dimension=0, tiled=True)
    rho_ij = lax.psum(local_channels, "grp")
    return (new_psi, density, rho_ij)


def solution(mesh):
    placed = (P("grp", "dom"), P("dom", None, None), P("dom"), P(), P(), P(), P())
    return jax.shard_map(
        on_device,
        mesh=mesh,
        in_specs=placed,
        out_specs=(P("grp", "dom"), P(("dom", "grp")), P()),
        check_vma=False,
    )
```

profile of v0, /device:TPU:1, one launch (start us, length us, event | category | flops | bytes accessed | tf_op | source)
XLA Modules:
  0.0 806.2 jit_solution(11860584338265138688)
XLA Ops:
  11.5 81.3 %all-gather.4.cloned.1.call-done = f32[1024,2048]{1,0:T(8,128)} async-done(((f32[64,2048]{1,0:T(8,128)}), f32[1024,2048]{1,0:T(8,128)}) %all-gather.4.cloned.1.call-update) | async-done | bytes 8388624 | tf_op jit(solution)/shard_map/all_gather | solution.py:35
  92.8 12.3 %fusion.87 = f32[64,1024]{1,0:T(8,128)} fusion(f32[64,2048]{1,0:T(8,128)} %param.7, f32[1024,2048]{1,0:T(8,128)} %all-gather.4.cloned.1.call-done), kind=kOutput, calls=%fused_computation.180 | convolution fusion | flops 1610612736 | bytes 9175040 | tf_op jit(solution)/shard_map/dot_general | solution.py:10
  105.2 124.6 %all-reduce.6.cloned.1.call-done = (f32[64,1024]{1,0:T(8,128)}, f32[64,1024]{1,0:T(8,128)}) async-done(((f32[64,1024]{1,0:T(8,128)}, f32[64,1024]{1,0:T(8,128)}), (f32[64,1024]{1,0:T(8,128)}, f32[64,1024]{1,0:T(8,128)})) %all-reduce.6.cloned.1.call-update) | async-done | bytes 524304 | tf_op jit(solution)/shard_map/psum | solution.py:40
  232.8 71.7 %all-gather.6.cloned.1.call-done = f32[1024,1024]{1,0:T(8,128)} async-done(((f32[64,1024]{1,0:T(8,128)}), f32[1024,1024]{1,0:T(8,128)}) %all-gather.6.cloned.1.call-update) | async-done | bytes 4194320 | tf_op jit(solution)/shard_map/all_gather | solution.py:36
  304.5 7.1 convolution_add_fusion
  313.7 58.1 %all-gather.8.cloned.1.call-done = f32[1024,1024]{1,0:T(8,128)} async-done(((f32[64,1024]{1,0:T(8,128)}), f32[1024,1024]{1,0:T(8,128)}) %all-gather.8.cloned.1.call-update) | async-done | bytes 4194320 | tf_op jit(solution)/shard_map/all_gather | solution.py:41
  371.8 5.9 copy.26
  377.7 4.4 fusion
  384.1 11.7 %cholesky.223 = f32[128,128]{1,0:T(8,128)S(1)} custom-call(f32[128,128]{1,0:T(8,128)S(1)} %cholesky.580), custom_call_target="Cholesky" | custom-call | tf_op jit(solution)/shard_map/jit(cholesky)/cholesky | solution.py:42
  398.3 9.8 %custom-call.62 = f32[1,128,128]{1,2,0:T(8,128)S(1)} custom-call(f32[1,128,128]{2,1,0:T(8,128)S(1)} %get-tuple-element.48), custom_call_target="InvertDiagBlocksLowerTriangular" | custom-call | tf_op jit(solution)/shard_map/jit(cholesky)/cholesky | solution.py:42
  412.0 11.9 %cholesky.244 = f32[128,128]{1,0:T(8,128)S(1)} custom-call(f32[128,128]{1,0:T(8,128)S(1)} %cholesky.584), custom_call_target="Cholesky" | custom-call | tf_op jit(solution)/shard_map/jit(cholesky)/cholesky | solution.py:42
  424.6 9.8 %custom-call.63 = f32[1,128,128]{1,2,0:T(8,128)S(1)} custom-call(f32[1,128,128]{2,1,0:T(8,128)S(1)} %get-tuple-element.45), custom_call_target="InvertDiagBlocksLowerTriangular" | custom-call | tf_op jit(solution)/shard_map/jit(cholesky)/cholesky | solution.py:42
  437.7 11.7 %cholesky.468 = f32[128,128]{1,0:T(8,128)S(1)} custom-call(f32[128,128]{1,0:T(8,128)S(1)} %cholesky.589), custom_call_target="Cholesky" | custom-call | tf_op jit(solution)/shard_map/jit(cholesky)/cholesky | solution.py:42
  450.8 9.8 %custom-call.64 = f32[1,128,128]{1,2,0:T(8,128)S(1)} custom-call(f32[1,128,128]{2,1,0:T(8,128)S(1)} %get-tuple-element.42), custom_call_target="InvertDiagBlocksLowerTriangular" | custom-call | tf_op jit(solution)/shard_map/jit(cholesky)/cholesky | solution.py:42
  464.1 11.9 %cholesky.487 = f32[128,128]{1,0:T(8,128)S(1)} custom-call(f32[128,128]{1,0:T(8,128)S(1)} %cholesky.594), custom_call_target="Cholesky" | custom-call | tf_op jit(solution)/shard_map/jit(cholesky)/cholesky | solution.py:42
  477.3 9.8 %custom-call.65 = f32[1,128,128]{1,2,0:T(8,128)S(1)} custom-call(f32[1,128,128]{2,1,0:T(8,128)S(1)} %get-tuple-element.39), custom_call_target="InvertDiagBlocksLowerTriangular" | custom-call | tf_op jit(solution)/shard_map/jit(cholesky)/cholesky | solution.py:42
  490.6 11.7 %cholesky.506 = f32[128,128]{1,0:T(8,128)S(1)} custom-call(f32[128,128]{1,0:T(8,128)S(1)} %cholesky.599), custom_call_target="Cholesky" | custom-call | tf_op jit(solution)/shard_map/jit(cholesky)/cholesky | solution.py:42
  503.6 10.2 %custom-call.66 = f32[1,128,128]{1,2,0:T(8,128)S(1)} custom-call(f32[1,128,128]{2,1,0:T(8,128)S(1)} %get-tuple-element.36), custom_call_target="InvertDiagBlocksLowerTriangular" | custom-call | tf_op jit(solution)/shard_map/jit(cholesky)/cholesky | solution.py:42
  517.0 11.7 %cholesky.526 = f32[128,128]{1,0:T(8,128)S(1)} custom-call(f32[128,128]{1,0:T(8,128)S(1)} %cholesky.604), custom_call_target="Cholesky" | custom-call | tf_op jit(solution)/shard_map/jit(cholesky)/cholesky | solution.py:42
  530.1 9.8 %custom-call.67 = f32[1,128,128]{1,2,0:T(8,128)S(1)} custom-call(f32[1,128,128]{2,1,0:T(8,128)S(1)} %get-tuple-element.33), custom_call_target="InvertDiagBlocksLowerTriangular" | custom-call | tf_op jit(solution)/shard_map/jit(cholesky)/cholesky | solution.py:42
  543.0 11.9 %cholesky.546 = f32[128,128]{1,0:T(8,128)S(1)} custom-call(f32[128,128]{1,0:T(8,128)S(1)} %cholesky.609), custom_call_target="Cholesky" | custom-call | tf_op jit(solution)/shard_map/jit(cholesky)/cholesky | solution.py:42
  556.2 9.8 %custom-call.68 = f32[1,128,128]{1,2,0:T(8,128)S(1)} custom-call(f32[1,128,128]{2,1,0:T(8,128)S(1)} %get-tuple-element.30), custom_call_target="InvertDiagBlocksLowerTriangular" | custom-call | tf_op jit(solution)/shard_map/jit(cholesky)/cholesky | solution.py:42
  568.6 11.7 %cholesky.564 = f32[128,128]{1,0:T(8,128)S(1)} custom-call(f32[128,128]{1,0:T(8,128)S(1)} %convolution_subtract_fusion.11), custom_call_target="Cholesky" | custom-call | tf_op jit(solution)/shard_map/jit(cholesky)/cholesky | solution.py:42
  587.3 4.8 select_select_fusion
  592.2 23.2 %while.1 = (s32[]{:T(128)}, f32[1024,1024]{1,0:T(8,128)}, s32[8,2]{0,1:T(2,128)S(1)}, f32[8,128,128]{2,1,0:T(8,128)S(1)}, s32[]{:T(128)}) while((s32[]{:T(128)}, f32[1024,1024]{1,0:T(8,128)}, s32[8,2]{0,1:T(2,128)S(1)}, f32[8,128,128]{2,1,0:T(8,128)S(1)}, s32[]{:T(128)}) %tuple.44), condition=%wide.while_cond, body=%wide.while_body.sunk | while | flops 2 | bytes 131181 | solution.py:43
  615.4 78.8 %custom-call.69 = f32[8,128,128]{1,2,0:T(8,128)S(1)} custom-call(f32[8,128,128]{2,1,0:T(8,128)S(1)} %get-tuple-element.10), custom_call_target="InvertDiagBlocksLowerTriangular" | custom-call | tf_op jit(solution)/shard_map/triangular_solve | solution.py:43
  706.4 2.7 convolution_subtract_fusion.2
  709.9 2.9 convolution_subtract_fusion.1
  713.7 3.6 convolution_subtract_fusion.3
  719.5 6.9 convolution_bitcast_fusion
  727.6 9.9 %fusion.33 = (f32[2048]{0:T(1024)S(1)}, f32[64,2048]{1,0:T(8,128)}) fusion(f32[64]{0:T(128)S(1)} %get-tuple-element.23, f32[1024,2048]{1,0:T(8,128)} %all-gather.4.cloned.1.call-done, f32[1024,1024]{1,0:T(8,128)} %copy-done.6, s32[]{:T(128)S(6)} %select_n.13), kind=kOutput, calls=%fused_computation.57 | convolution fusion | flops 1611003904 | bytes 9445636 | tf_op jit(solution)/shard_map/dot_general | solution.py:10
  737.5 61.4 %all-reduce.2 = (f32[2048]{0:T(1024)S(1)}, f32[128,64]{0,1:T(8,128)}) all-reduce(f32[2048]{0:T(1024)S(1)} %broadcast_multiply_fusion, f32[128,64]{0,1:T(8,128)S(1)} %bitcast.120), channel_id=2, replica_groups=mesh['dom'=16,'grp'=16] {'grp'}, use_global_device_ids=true, to_apply=%region_19.20.clone | all-reduce | flops 10240 | bytes 81920
  (139 shorter events, 85.5 us)
Async XLA Ops:
  7.2 1.4 copy-start
  7.2 85.7 %all-gather.4.cloned.1.call-start = ((), (), s32[]{:S(2)}) async-start(), calls=%async_computation | async-start | bytes 8912896 | tf_op jit(solution)/shard_map/all_gather | solution.py:35
  7.9 221.9 %all-reduce.6.cloned.1.call-start = ((), (), s32[]{:S(2)}) async-start(), calls=%async_computation.3 | async-start | bytes 1048576 | tf_op jit(solution)/shard_map/psum | solution.py:40
  11.5 93.6 %copy-start.5 = (f32[64,1024]{1,0:T(8,128)}, f32[64,1024]{1,0:T(8,128)S(1)}, u32[]{:S(2)}) copy-start(f32[64,1024]{1,0:T(8,128)S(1)} %dynamic_update_slice.3) | copy-start | bytes 786436
  11.5 218.7 %copy-start.7 = (f32[4,8,8]{2,1,0:T(8,128)S(1)}, f32[4,8,8]{2,1,0:T(8,128)}, u32[]{:S(2)}) copy-start(f32[4,8,8]{2,1,0:T(8,128)} %param.11) | copy-start | bytes 3076
  11.5 218.7 %copy-start.8 = (s32[128]{0:T(128)S(1)}, s32[128]{0:T(128)}, u32[]{:S(2)}) copy-start(s32[128]{0:T(128)} %param.10) | copy-start | bytes 1540
  105.1 199.4 %all-gather.6.cloned.1.call-start = ((), (), s32[]{:S(2)}) async-start(), calls=%async_computation.1 | async-start | bytes 4456448 | tf_op jit(solution)/shard_map/all_gather | solution.py:36
  229.8 142.0 %all-gather.8.cloned.1.call-start = ((), (), s32[]{:S(2)}) async-start(), calls=%async_computation.2 | async-start | bytes 4456448 | tf_op jit(solution)/shard_map/all_gather | solution.py:41
  230.4 81.3 %copy-start.9 = (u32[256]{0:T(256)S(1)}, u32[256]{0:T(256)}, u32[]{:S(2)}) copy-start(u32[256]{0:T(256)} %constant.314) | copy-start | bytes 3076
  382.1 2.0 copy-start.3
  694.2 6.5 copy-start.4
  717.3 2.2 copy-start.2
  719.5 6.9 copy-start.6
  727.6 71.8 %copy-start.1 = (f32[1,128,2048]{2,1,0:T(8,128)S(1)}, f32[1,128,2048]{2,1,0:T(8,128)}, u32[]{:S(2)}) copy-start(f32[1,128,2048]{2,1,0:T(8,128)} %param.8) | copy-start | bytes 3145732
Sparse Core Ops, SparseCore 0:
  10.8 82.0 all-gather.3
  105.2 124.5 all-reduce.5
  232.9 71.5 all-gather.5
  311.8 59.9 all-gather.7
where the time goes:
time: 818 us; the launch traced here: 806 us
  waiting for transfers between devices  336 us (41%)
  other arithmetic  261 us (32%)
  matrix products  86.6 us (11%)
  blocking collectives  61.4 us (8%)
  local copies, waits for them, and re-layouts  38.9 us (5%)
  between operations  21 us (3%)
    another operation x30, other arithmetic, on_device(): lower = jnp.linalg.cholesky(gram)  172 us
    psum x1, waiting for transfers between devices, on_device(): gram_rows_own = lax.psum(grid_part, 'dom') + paw_part  125 us
    another operation x3, other arithmetic, on_device(): lax.linalg.triangular_solve(lower, rotation, left_side=True, lower=True,...  83.6 us
    all_gather x1, waiting for transfers between devices, on_device(): lax.all_gather(psi, 'grp', axis=0, tiled=True)  81.3 us
    all_gather x1, waiting for transfers between devices, on_device(): lax.all_gather(coeff, 'grp', axis=0, tiled=True)  71.7 us
    unnamed x1, blocking collectives  61.4 us
    all_gather x1, waiting for transfers between devices, on_device(): gram = lax.all_gather(gram_rows_own, 'grp', axis=0, tiled=True)  58.1 us
    dot_general x5, matrix products, product(): jnp.dot(left, right, precision=highest, preferred_element_type=jnp.float32)  38.4 us
  transfers between devices with their start and end apart: 4, of which 4 were waited for; matrix products, arithmetic and copies ran while one was open for 1% of the time, Pallas kernels for 0%

commit v1 on v0

v1 whole, which is shorter than its diff:
```python
import functools
import jax, jax.numpy as jnp
from jax import lax
from jax.experimental import pallas as pl
from jax.experimental.pallas import tpu as pltpu
from jax.sharding import PartitionSpec as P
f32, bf16 = jnp.float32, jnp.bfloat16
NB=8
def split(x):
    hi = x.astype(bf16)
    return hi, (x - hi.astype(f32)).astype(bf16)
def nt(a, b):
    return lax.dot_general(a, b, (((1,),(1,)),((),())), preferred_element_type=f32)
def nn(a, b):
    return jnp.dot(a, b, preferred_element_type=f32)
def dot3(f, a, b):
    return f(a[0], b[0]) + (f(a[0], b[1]) + f(a[1], b[0]))

def lane_b(v, c): return jnp.broadcast_to(v[:, c:c+1], (8,128))
def row_b(v, s): return jnp.broadcast_to(v[s:s+1, :], (8,128))

def diag(V, hook):
    V = list(V)
    row = lax.broadcasted_iota(jnp.int32, (8,128), 0)
    lane = lax.broadcasted_iota(jnp.int32, (8,128), 1)
    Wp = [jnp.where(lane == row + 8*i, 1.0, 0.0).astype(f32) for i in range(16)]
    out = []
    for j in range(16):
        C = {i: [lane_b(V[i], 8*j+t) for t in range(8)] for i in range(j, 16)}
        D = {(s,t): row_b(C[j][t], s) for t in range(8) for s in range(t, 8)}
        RA = [row_b(V[j], t) for t in range(8)]
        RW = [row_b(Wp[j], t) for t in range(8)]
        for t0 in range(0, 8, 2):
            t1 = t0+1
            a, b, c = D[t0,t0], D[t1,t0], D[t1,t1]
            det = a*c - b*b
            r0 = 1.0/a
            rd = 1.0/det
            r1 = a*rd
            for t, r in ((t0,r0),(t1,r1)):
                l = {s: D[s,t]*r for s in range(t+1,8)}
                for s in range(t+1,8):
                    for u in range(t+1,s+1):
                        if s==u==t1 and t==t0: continue
                        D[s,u] = D[s,u] - l[s]*D[u,t]
                for s in range(t+1,8):
                    RA[s] = RA[s] - l[s]*RA[t]
                    RW[s] = RW[s] - l[s]*RW[t]
                for i in range(j+1,16):
                    li = C[i][t]*r
                    for u in range(t+1,8):
                        C[i][u] = C[i][u] - li*D[u,t]
                    V[i] = V[i] - li*RA[t]
                    Wp[i] = Wp[i] - li*RW[t]
            D[t1,t1] = det*r0
        w = RW[0]*lax.rsqrt(D[0,0])
        for t in range(1,8):
            w = jnp.where(row==t, RW[t]*lax.rsqrt(D[t,t]), w)
        out.append(w)
        hook()
    return jnp.concatenate(out, axis=0)

def kern(s_ref, b_ref, y_ref, A, B):
    A[...] = s_ref[...]
    B[...] = b_ref[...]
    pending = []
    def hook():
        if pending: pending.pop(0)()
    for k in range(NB):
        r = pl.ds(128*k, 128)
        W = diag([A[128*k+8*i:128*k+8*i+8, 128*k:128*k+128] for i in range(16)], hook)
        while pending: hook()
        Wp = split(W)
        Bk = split(B[r, :])
        Y = dot3(nn, Wp, Bk)
        y_ref[r, :] = Y
        if k == NB-1: break
        L = dot3(nt, split(A[128*(k+1):, 128*k:128*k+128]), Wp)
        Lp = split(L)
        Yp = split(Y)
        def upd(c, k=k, Lp=Lp):
            o = 128*(c-k-1)
            Lc = tuple(x[o:o+128] for x in Lp)
            Lr = tuple(x[o:] for x in Lp)
            A[128*c:, 128*c:128*c+128] -= dot3(nt, Lr, Lc)
        def updB(i, k=k, Lp=Lp, Yp=Yp):
            o = 128*(i-k-1)
            B[128*i:128*i+128, :] -= dot3(nn, tuple(x[o:o+128] for x in Lp), Yp)
        o=0
        A[128*(k+1):128*(k+2), 128*(k+1):128*(k+2)] -= dot3(nt, tuple(x[:128] for x in Lp), tuple(x[:128] for x in Lp))
        def upd0(k=k, Lp=Lp):
            if k+2 < NB:
                A[128*(k+2):, 128*(k+1):128*(k+2)] -= dot3(nt, tuple(x[128:] for x in Lp), tuple(x[:128] for x in Lp))
        pending.append(upd0)
        for c in range(k+2, NB): pending.append(functools.partial(upd, c))
        for i in range(k+1, NB): pending.append(functools.partial(updB, i))

def cholsolve(s, b):
    n, m = b.shape
    return pl.pallas_call(kern, out_shape=jax.ShapeDtypeStruct((n,m), f32),
        in_specs=[pl.BlockSpec(memory_space=pltpu.VMEM)]*2, out_specs=pl.BlockSpec(memory_space=pltpu.VMEM),
        scratch_shapes=[pltpu.VMEM((n,n), f32), pltpu.VMEM((n,m), f32)],
        compiler_params=pltpu.CompilerParams(vmem_limit_bytes=48*2**20))(s, b)


highest = lax.Precision.HIGHEST


def on_device(psi, proj, offsets, species, augment_q, rotation, occupation):
    states, cells = psi.shape
    groups, doms = lax.axis_size("grp"), lax.axis_size("dom")
    kinds, channels, _ = augment_q.shape
    atoms = species.shape[0]
    total, own_cells, own_atoms = states*groups, cells//groups, atoms//doms
    part = psi.reshape(states, groups, own_cells)
    psi_c = lax.all_to_all(part, "grp", 1, 0, tiled=True).reshape(total, own_cells)
    partial = jnp.dot(psi, proj[0].T, precision=highest)
    placed = lax.dynamic_update_slice(
        jnp.zeros((states, atoms*channels), f32), partial, (jnp.int32(0), offsets[0]*channels))
    mine = lax.psum_scatter(placed, "dom", scatter_dimension=1, tiled=True)
    coeff = lax.all_gather(mine, "grp", axis=0, tiled=True)
    first = lax.axis_index("dom")*own_atoms
    kind = lax.dynamic_slice_in_dim(species, first, own_atoms, 0)
    table = (kind[:, None] == jnp.arange(kinds, dtype=jnp.int32)[None, :]).astype(f32)
    per_atom = jnp.einsum("as,sij->aij", table, augment_q, precision=highest)
    weighted = jnp.einsum("nai,aij->naj", coeff.reshape(total, own_atoms, channels), per_atom, precision=highest)
    weighted = weighted.reshape(total, -1) * (1.0/groups)
    left = jnp.concatenate([psi_c, weighted], axis=1)
    right = jnp.concatenate([psi_c, coeff], axis=1)
    gram = lax.psum(jnp.dot(left, right.T, precision=highest), ("dom", "grp"))
    both = jnp.concatenate([psi_c, coeff, jnp.zeros((total, 256-own_cells-coeff.shape[1]), f32)], axis=1)
    half = cholsolve(gram, both)
    new = jnp.dot(rotation.T, half, precision=highest)
    new_c = new[:, :own_cells]
    density = jnp.sum((occupation/total)[:, None]*new_c*new_c, axis=0)*(cells*doms)
    shaped = new[:, own_cells:own_cells+own_atoms*channels].reshape(total, own_atoms, channels)
    rho = jnp.einsum("n,nai,naj->aij", occupation, shaped, shaped, precision=highest).reshape(own_atoms, channels*channels)
    rho = lax.all_gather(rho, "dom", axis=0, tiled=True)
    back = lax.all_to_all(new_c.reshape(groups, states, own_cells), "grp", 0, 1, tiled=False)
    return back.reshape(states, cells), density, rho


def solution(mesh):
    placed = (P("grp", "dom"), P("dom", None, None), P("dom"), P(), P(), P(), P())
    return jax.shard_map(
        on_device, mesh=mesh, in_specs=placed,
        out_specs=(P("grp", "dom"), P(("dom", "grp")), P()), check_vma=False)
```

time: 818 us -> 489 us (0.60)
  the two profiles are of different devices: /device:TPU:1 before, /device:TPU:4 now
where the time goes in v1:
time: 489 us; the launch traced here: 485 us
  waiting for transfers between devices  332 us (68%)
  blocking collectives  54.6 us (11%)
  Pallas kernels  47 us (10%)
  between operations  15.2 us (3%)
  starting transfers between devices  14.3 us (3%)
  matrix products  12.7 us (3%)
  local copies, waits for them, and re-layouts  8.36 us (2%)
    psum x1, waiting for transfers between devices, on_device(): gram = lax.psum(jnp.dot(left, right.T, precision=highest), ('dom', 'grp'))  268 us
    unnamed x3, waiting for transfers between devices  63.8 us
    pallas_call x1, Pallas kernels, cholsolve(): pl.pallas_call(kern, out_shape=jax.ShapeDtypeStruct((n, m), f32), in_spec...  47 us
    all_gather x1, blocking collectives, on_device(): rho = lax.all_gather(rho, 'dom', axis=0, tiled=True)  33.1 us
    all_gather x1, blocking collectives, on_device(): coeff = lax.all_gather(mine, 'grp', axis=0, tiled=True)  21.6 us
  transfers between devices with their start and end apart: 4, of which 2 were waited for; matrix products, arithmetic and copies ran while one was open for 1% of the time, Pallas kernels for 0%

profile of v1, /device:TPU:4, one launch (start us, length us, event | category | flops | bytes accessed | tf_op | source)
XLA Modules:
  0.0 484.8 jit_solution(11379947240389279007)
XLA Ops:
  7.2 0.0 reduce-scatter.4.cloned.1.call-start
  8.0 0.4 copy-done
  8.4 2.2 fusion.4
  10.7 0.6 dynamic_update_slice.3
  11.3 1.0 copy.37
  12.3 1.9 copy_bitcast_fusion.1
  14.2 7.5 %all-to-all-start = ((f32[64,16,128]{2,0,1:T(8,128)}), f32[64,16,128]{2,0,1:T(8,128)S(1)}, u32[]{:S(2)}, u32[]{:S(2)}) async-start(f32[64,16,128]{2,0,1:T(8,128)} %copy_bitcast_fusion.1), calls=%async_computation | async-start | bytes 1048576 | tf_op jit(solution)/shard_map/all_to_all | solution.py:116
  21.7 0.0 all-reduce.2.cloned.1.call-start
  21.7 0.1 dynamic_slice.3
  21.8 0.2 fusion.12
  22.0 63.7 %reduce-scatter.4.cloned.1.call-done = f32[64,64]{1,0:T(8,128)} async-done(((f32[1024,64]{1,0:T(8,128)}), f32[64,64]{1,0:T(8,128)}) %reduce-scatter.4.cloned.1.call-update) | async-done | bytes 16400
  85.7 0.8 copy.38
  86.6 21.6 %all_gather.6 = f32[1024,64]{1,0:T(8,128)S(1)} all-gather(f32[64,64]{1,0:T(8,128)S(1)} %copy.38), channel_id=1, replica_groups=mesh['dom'=16,'grp'=16] {'grp'}, dimensions={0}, use_global_device_ids=true | all-gather | bytes 278528 | tf_op jit(solution)/shard_map/all_gather | solution.py:121
  108.1 0.2 copy.30
  108.3 0.4 fusion
  108.7 0.2 copy.32
  109.0 5.6 %fusion.1 = f32[1024,1024]{1,0:T(8,128)} fusion(f32[1024,128]{1,0:T(8,128)S(1)} %bitcast.48, f32[1024,64]{1,0:T(8,128)S(1)} %copy.32, f32[1024,64]{1,0:T(8,128)S(1)} %all_gather.6), kind=kOutput, calls=%fused_computation.5 | convolution fusion | flops 2416312320 | bytes 5242880 | tf_op jit(solution)/shard_map/dot_general | solution.py:130
  114.6 0.1 pad.2.clone
  114.7 0.1 maximum_maximum_fusion.b_ref
  114.8 268.1 %all-reduce.2.cloned.1.call-done.s_ref = f32[1024,1024]{1,0:T(8,128)} async-done(((f32[1024,1024]{1,0:T(8,128)}), f32[1024,1024]{1,0:T(8,128)}) %all-reduce.2.cloned.1.call-update) | async-done | bytes 4194320 | tf_op jit(solution)/shard_map/psum | solution.py:130
  382.9 47.0 %shard_map.94 = f32[1024,256]{1,0:T(8,128)S(1)} custom-call(f32[1024,1024]{1,0:T(8,128)} %all-reduce.2.cloned.1.call-done.s_ref, f32[1024,256]{1,0:T(8,128)S(1)} %maximum_maximum_fusion.b_ref), custom_call_target="tpu_custom_call" | custom-call | tf_op jit(solution)/shard_map/pallas_call | solution.py:100
  429.9 3.6 convolution_bitcast_fusion
  433.5 0.1 fusion.6
  433.7 1.0 copy.33
  434.7 6.7 %all-to-all-start.1 = ((f32[16,64,1,128]{3,1,2,0:T(8,128)}), f32[16,64,1,128]{3,1,2,0:T(8,128)S(1)}, u32[]{:S(2)}, u32[]{:S(2)}) async-start(f32[16,64,1,128]{3,1,2,0:T(8,128)} %bitcast.13), calls=%async_computation.1 | async-start | bytes 1048576 | tf_op jit(solution)/shard_map/all_to_all | solution.py:139
  441.4 0.6 fusion.7
  442.0 0.1 reshape.34
  442.1 33.1 %all_gather.7 = f32[128,64]{1,0:T(8,128)S(1)} all-gather(f32[8,64]{1,0:T(8,128)S(1)} %reshape.34), channel_id=1, replica_groups=mesh['dom'=16,'grp'=16] {'dom'}, dimensions={0}, use_global_device_ids=true | all-gather | bytes 34816 | tf_op jit(solution)/shard_map/all_gather | solution.py:138
  475.2 0.7 copy.36
  475.9 0.5 broadcast_multiply_fusion.1
  476.4 0.3 copy.35
  476.7 1.0 copy.47
  (16 shorter events, 0.1 us)
Async XLA Ops:
  7.2 1.2 copy-start
  7.2 14.5 %copy-start.4 = (s32[128]{0:T(128)S(1)}, s32[128]{0:T(128)}, u32[]{:S(2)}) copy-start(s32[128]{0:T(128)} %param.10) | copy-start | bytes 1540
  7.2 14.6 %copy-start.3 = (f32[4,8,8]{2,1,0:T(8,128)S(1)}, f32[4,8,8]{2,1,0:T(8,128)}, u32[]{:S(2)}) copy-start(f32[4,8,8]{2,1,0:T(8,128)} %param.11) | copy-start | bytes 3076
  7.2 78.5 %reduce-scatter.4.cloned.1.call-start = ((), (), s32[]{:S(2)}) async-start(), calls=%async_computation.4 | async-start | bytes 557056
  14.2 94.7 %all-to-all-start = ((f32[64,16,128]{2,0,1:T(8,128)}), f32[64,16,128]{2,0,1:T(8,128)S(1)}, u32[]{:S(2)}, u32[]{:S(2)}) async-start(f32[64,16,128]{2,0,1:T(8,128)} %copy_bitcast_fusion.1), calls=%async_computation | async-start | bytes 1048576 | tf_op jit(solution)/shard_map/all_to_all | solution.py:116
  21.7 361.3 %all-reduce.2.cloned.1.call-start = ((), (), s32[]{:S(2)}) async-start(), calls=%async_computation.3 | async-start | bytes 8388608 | tf_op jit(solution)/shard_map/psum | solution.py:130
  109.0 5.7 %copy-start.2 = (f32[1024]{0:T(1024)S(1)}, f32[1024]{0:T(1024)}, u32[]{:S(2)}) copy-start(f32[1024]{0:T(1024)} %param.13) | copy-start | bytes 12292
  382.9 47.0 %copy-start.1 = (f32[1024,1024]{1,0:T(8,128)S(1)}, f32[1024,1024]{1,0:T(8,128)}, u32[]{:S(2)}) copy-start(f32[1024,1024]{1,0:T(8,128)} %param.12) | copy-start | bytes 12582916
  434.7 41.7 %all-to-all-start.1 = ((f32[16,64,1,128]{3,1,2,0:T(8,128)}), f32[16,64,1,128]{3,1,2,0:T(8,128)S(1)}, u32[]{:S(2)}, u32[]{:S(2)}) async-start(f32[16,64,1,128]{3,1,2,0:T(8,128)} %bitcast.13), calls=%async_computation.1 | async-start | bytes 1048576 | tf_op jit(solution)/shard_map/all_to_all | solution.py:139
Sparse Core Ops, SparseCore 0:
  12.4 73.2 reduce-scatter.3
  114.7 268.1 all-reduce.1

commit v2 on v0

v2 whole, which is shorter than its diff:
```python
import functools
import jax
import jax.numpy as jnp
from jax import lax
from jax.experimental import pallas as pl
from jax.experimental.pallas import tpu as pltpu
from jax.sharding import PartitionSpec as P

f32, bf16 = jnp.float32, jnp.bfloat16
MESH = pl.DeviceIdType.MESH
NB = 8
BLK = 128
TOTAL = NB * BLK
UNIT = 64
START = [sum(NB - j for j in range(c)) for c in range(NB + 1)]
HALF = START[NB] * UNIT
CHUNK = (4, 16, 16)
CH = [u * UNIT for u in CHUNK]
CO = [sum(CH[:c]) for c in range(len(CH) + 1)]
PAD = 10


def split(v):
    hi = v.astype(bf16)
    return hi, (v - hi.astype(f32)).astype(bf16)


def nt(a, b):
    return lax.dot_general(a, b, (((1,), (1,)), ((), ())), preferred_element_type=f32)


def nn(a, b):
    return jnp.dot(a, b, preferred_element_type=f32)


def dot3(f, a, b):
    return f(a[0], b[0]) + (f(a[0], b[1]) + f(a[1], b[0]))


def dot3_nt(a, b):
    high = b[:, :BLK]
    return nt(a, jnp.concatenate([high, high], axis=1)) + nt(a[:, :BLK], b[:, BLK:])


def dot3_nn(a, b):
    return nn(a, jnp.concatenate([b[0], b[0]], axis=0)) + nn(a[:, :BLK], b[1])


def join(v):
    return jnp.concatenate(split(v), axis=1)


def rows(first, count, unit=8):
    return pl.ds(pl.multiple_of(first, unit), count)


class Place:
    def __init__(self):
        self.d, self.g = lax.axis_index("dom"), lax.axis_index("grp")
        self.core, self.chip = lax.rem(self.g, 2), self.g // 2

    def dom(self, i):
        return {"dom": i, "grp": self.g}

    def grp(self, i):
        return {"dom": self.d, "grp": i}

    def other_core(self):
        return self.grp(self.g + 1 - 2 * self.core)


def greet(me):
    barrier = pltpu.get_barrier_semaphore()

    def one(p, carry):
        pl.semaphore_signal(barrier, inc=1, device_id=me.grp(lax.rem(me.g + p, 16)), device_id_type=MESH)
        pl.semaphore_signal(barrier, inc=1, device_id=me.dom(lax.rem(me.d + p, 16)), device_id_type=MESH)
        return carry

    lax.fori_loop(1, 16, one, 0)
    pl.semaphore_wait(barrier, 30)


def remote(src, dst, send, recv, device):
    return pltpu.make_async_remote_copy(
        src_ref=src, dst_ref=dst, send_sem=send, recv_sem=recv, device_id=device, device_id_type=MESH)


def row_b(v, s):
    return jnp.broadcast_to(v[s:s + 1, :], (8, BLK))


def recip(a):
    r = pl.reciprocal(a, approx=True)
    return r * (2.0 - a * r)


def inverse_factor(V, hook):
    row = lax.broadcasted_iota(jnp.int32, (8, BLK), 0)
    where = lax.broadcasted_iota(jnp.int32, (16, 8, BLK), 0) * 8 + lax.broadcasted_iota(jnp.int32, (16, 8, BLK), 1)
    W = jnp.where(lax.broadcasted_iota(jnp.int32, (16, 8, BLK), 2) == where, 1.0, 0.0).astype(f32)
    out = []
    for j in range(16):
        col = [jnp.broadcast_to(V[:, :, 8 * j + t:8 * j + t + 1], V.shape) for t in range(8)]
        D = {(s, t): row_b(col[t][0], s) for t in range(8) for s in range(t, 8)}
        RA = [row_b(V[0], t) for t in range(8)]
        RW = [row_b(W[0], t) for t in range(8)]
        scale = []
        more = j < 15
        if more:
            C = [c[1:] for c in col]
            V, W = V[1:], W[1:]
        for t0 in range(0, 8, 2):
            t1 = t0 + 1
            a, b, c = D[t0, t0], D[t1, t0], D[t1, t1]
            det = a * c - b * b
            r0 = recip(a)
            r1 = a * recip(det)
            D[t1, t1] = det * r0
            scale += [lax.rsqrt(a), lax.rsqrt(D[t1, t1])]
            for t, r in ((t0, r0), (t1, r1)):
                l = {s: D[s, t] * r for s in range(t + 1, 8)}
                for s in range(t + 1, 8):
                    for u in range(t + 1, s + 1):
                        if not (s == t1 and t == t0):
                            D[s, u] = D[s, u] - l[s] * D[u, t]
                for s in range(t + 1, 8):
                    RA[s] = RA[s] - l[s] * RA[t]
                    RW[s] = RW[s] - l[s] * RW[t]
                if more:
                    li = C[t] * r[None]
                    for u in range(t + 1, 8):
                        C[u] = C[u] - li * D[u, t][None]
                    V = V - li * RA[t][None]
                    W = W - li * RW[t][None]
        w = RW[0] * scale[0]
        for t in range(1, 8):
            w = jnp.where(row == t, RW[t] * scale[t], w)
        out.append(w)
        hook()
    return jnp.concatenate(out, axis=0)


def kernel(psi, proj, off, species, aug, rot, occ, out, dens, all_rho,
           psi_v, proj_v, rot_v, rt, placed, got, cp, pc, cf, ps, cs, ws, tiled, t, tp, rc, h, r1, q1, r2, o,
           A, B, L, YH, YL, zp, zc, own_rho,
           s_in, s_psi, r_psi, s_dom, r_dom, s_cf, r_cf, s_core, r_core, s_x, r_x, s_z, r_z, s_new, r_new, s_rho, r_rho):
    me = Place()
    loads = [pltpu.make_async_copy(src, dst, s_in.at[i])
             for i, (src, dst) in enumerate(((psi, psi_v), (proj, proj_v), (rot, rot_v)))]
    for load in loads:
        load.start()
    greet(me)
    own = rows(me.g * UNIT, UNIT)

    def psi_copy(p, to):
        return remote(psi.at[:, rows(to * BLK, BLK, BLK)], pc.at[own, :], s_psi.at[p], r_psi.at[p], me.grp(to))

    def dom_copy(p, to):
        return remote(placed.at[to], got.at[p], s_dom.at[p], r_dom.at[p], me.dom(to))

    def cf_copy(p, to):
        return remote(cp.at[me.g], cp.at[me.g], s_cf.at[p], r_cf.at[p], me.grp(to))

    def each(body):
        def one(p, carry):
            body(p)
            return carry
        lax.fori_loop(1, 16, one, 0)

    each(lambda p: psi_copy(p, lax.rem(me.g + p, 16)).start())

    loads[0].wait()
    loads[1].wait()
    pc[own, :] = psi_v[:, rows(me.g * BLK, BLK, BLK)]
    value = dot3(nt, split(psi_v[...]), split(proj_v[0]))
    value = split(jnp.concatenate([value[:32], value[32:]], axis=1))
    source = lax.broadcasted_iota(jnp.int32, (2 * BLK, BLK), 0)
    lane = lax.broadcasted_iota(jnp.int32, (2 * BLK, BLK), 1)
    gap = jnp.where((source < BLK) == (lane < UNIT), lax.rem(source, BLK) - lax.rem(lane, UNIT), -4096) + off[0] * 8
    for d in range(16):
        pick = jnp.where(gap == UNIT * d, 1.0, 0.0).astype(bf16)
        placed[d] = nn(value[0], pick) + nn(value[1], pick)
    each(lambda p: dom_copy(p, lax.rem(me.d + p, 16)).start())

    A[...] = jnp.zeros(A.shape, f32)
    B[pl.ds(TOTAL, (PAD - NB) * BLK), :] = jnp.zeros(((PAD - NB) * BLK, 2 * BLK), f32)
    lane = lax.broadcasted_iota(jnp.int32, (8, BLK), 1)
    repeat = jnp.where(lax.broadcasted_iota(jnp.int32, (8, BLK), 0) == lax.rem(lane, 8), 1.0, 0.0)
    tiled[...] = jnp.dot(aug[...].reshape(32, 8), repeat, precision=lax.Precision.HIGHEST).reshape(4, 8, BLK)
    blocks = [jnp.where(lane // 8 == a, tiled[species[me.d * 8 + a]], 0.0) for a in range(8)]
    blocks.append(jnp.zeros((UNIT, BLK), f32))
    q = split(jnp.concatenate(blocks, axis=0))
    loads[2].wait()

    def turn(i, carry):
        hi, lo = split(rot_v[rows(i * BLK, BLK, BLK), :].T)
        rt[0, :, rows(i * BLK, BLK, BLK)] = hi
        rt[1, :, rows(i * BLK, BLK, BLK)] = lo
        return carry

    lax.fori_loop(0, NB, turn, 0)

    def add_dom(p, total):
        dom_copy(p, me.d).wait_recv()
        return total + got[p]

    started = []
    waits = {}

    def go(copy):
        copy.start()
        started.append(copy)
        return copy

    def arrive(key):
        for copy in waits[key]:
            copy.wait_recv()

    def spread(n, mine, device, source, target, s_sem, r_sem):
        copies = []
        for p in range(1, n):
            to = lax.rem(mine + p, n)
            copies.append(go(remote(source(to), target, s_sem.at[p], r_sem.at[p], device(to))))
        return copies

    def chips(c, i, source, target):
        return spread(8, me.chip, lambda to: me.grp(to * 2 + me.core), source, target, s_x.at[c, i], r_x.at[c, i])

    def doms(c, i, source, target):
        return spread(16, me.d, me.dom, source, target, s_z.at[c, i], r_z.at[c, i])

    def sizes(c):
        return CO[c], CH[c], CO[c] // 8, CH[c] // 8

    def step_a(c):
        chunk = pl.ds(CO[c], CH[c])
        waits["a", c] = [go(remote(t.at[1 - me.core, chunk], rc.at[chunk], s_core.at[c], r_core.at[c], me.other_core()))]

    def step_b(c):
        arrive(("a", c))
        first, count, at, n = sizes(c)
        chunk = pl.ds(first, count)
        h[chunk] = t[me.core, chunk] + rc[chunk]
        waits["b", c] = chips(c, 0, lambda to: h.at[rows(first + to * n, n)], r1.at[me.chip, pl.ds(at, n)])

    def step_c(c):
        arrive(("b", c))
        first, count, at, n = sizes(c)
        mine, part = rows(first + me.chip * n, n), pl.ds(at, n)
        r1[me.chip, part] = h[mine] + tp[mine]
        total = r1[0, part]
        for i in range(1, 8):
            total = total + r1[i, part]
        if c == 0:
            r2[me.d, part] = total
            waits["c", c] = doms(c, 0, lambda to: r2.at[me.d, part], r2.at[me.d, part])
        else:
            q1[part] = total
            m = n // 16
            waits["c", c] = doms(c, 0, lambda to: q1.at[rows(at + to * m, m)], r2.at[me.d, pl.ds(at, m)])

    def step_d(c):
        arrive(("c", c))
        first, count, at, n = sizes(c)
        if c == 0:
            part, here = pl.ds(at, n), o.at[me.core, rows(first + me.chip * n, n)]
        else:
            m = n // 16
            part, here = pl.ds(at, m), o.at[me.core, rows(first + me.chip * n + me.d * m, m)]
            r2[me.d, part] = q1[rows(at + me.d * m, m)]
        total = r2[0, part]
        for i in range(1, 16):
            total = total + r2[i, part]
        here[...] = total
        if c:
            waits["d", c] = doms(c, 1, lambda to: here, here)

    def step_e(c):
        if c:
            arrive(("d", c))
        first, count, at, n = sizes(c)
        here = o.at[me.core, rows(first + me.chip * n, n)]
        waits["e", c] = chips(c, 1, lambda to: here, here)

    def step_f(c):
        arrive(("e", c))
        here = o.at[me.core, pl.ds(CO[c], CH[c])]
        n = len(CHUNK) + c
        waits["f", c] = [go(remote(here, here, s_core.at[n], r_core.at[n], me.other_core()))]

    def step_g(c):
        arrive(("f", c))
        for col in range(NB):
            for r in range(NB - col):
                unit = START[col] + r
                if CO[c] <= unit * UNIT < CO[c + 1]:
                    for half in range(2):
                        A[col, BLK * r + UNIT * half:BLK * r + UNIT * half + UNIT] += o[half, pl.ds(unit * UNIT, UNIT)]

    def do(*names):
        for name in names:
            {"a": step_a, "b": step_b, "c": step_c, "d": step_d, "e": step_e, "f": step_f, "g": step_g}[name[0]](int(name[1]))

    def gram_of_psi():
        ready = 0
        for c in range(NB):
            part = dot3_nt(ps[BLK * c:], ps[BLK * c:BLK * c + BLK])
            for r in range(NB - c):
                for half in range(2):
                    t[half, pl.ds(UNIT * (START[c] + r), UNIT)] = part[BLK * r + UNIT * half: BLK * r + UNIT * half + UNIT]
            while ready < len(CHUNK) and CO[ready + 1] <= START[c + 1] * UNIT:
                step_a(ready)
                ready += 1

    cp[me.g] = lax.fori_loop(1, 16, add_dom, placed[me.d])
    each(lambda p: cf_copy(p, lax.rem(me.g + p, 16)).start())

    each(lambda p: psi_copy(p, me.g).wait_recv())
    ps[...] = join(pc[...])
    gram_of_psi()
    do("b0", "b1")
    B[:TOTAL, :BLK] = pc[...]

    each(lambda p: cf_copy(p, me.g).wait_recv())
    left = lax.broadcasted_iota(jnp.int32, (32, BLK), 1) < UNIT
    for g in range(16):
        cf[UNIT * g:UNIT * g + 32] = jnp.where(left, cp[g], 0.0)
        cf[UNIT * g + 32:UNIT * g + 64] = jnp.where(left, pltpu.roll(cp[g], UNIT, 1), 0.0)
    cs[...] = join(cf[...])
    ws[...] = join(dot3(nn, split(cf[...]), q)).reshape(NB, 2, UNIT, 2 * BLK)
    for c in range(NB):
        own_rows = ws[c:, me.core].reshape((NB - c) * UNIT, 2 * BLK)
        tp[pl.ds(START[c] * UNIT, (NB - c) * UNIT)] = dot3_nt(own_rows, cs[BLK * c:BLK * c + BLK])
    do("c0", "b2")
    B[:TOTAL, BLK:] = cf[...]
    do("c1", "d0", "e0", "c2", "d1", "f0", "d2", "e1", "g0")

    def add_new(i, k):
        piece, past = pl.ds(2 * BLK * i, 2 * BLK), rows(k * BLK, BLK, BLK)
        new = dot3_nn(jnp.concatenate([rt[0, piece, past], rt[1, piece, past]], axis=1), (YH[...], YL[...]))
        zp[piece] += new[:, :BLK]
        zc[piece] += new[:, BLK:]

    def step(k, m, first=False, extra=None, last=()):
        work = []

        def column(b):
            n = max(m - b, 0) if b else m - 1
            a = b if b else 1
            A[k + b, pl.ds(BLK * (a - b), BLK * n), :] -= dot3_nt(L[pl.ds(BLK * a, BLK * n), :], L[pl.ds(BLK * b, BLK), :])

        def right(a):
            B[rows((k + a) * BLK, BLK), :] -= dot3_nn(L[pl.ds(BLK * a, BLK), :], (YH[...], YL[...]))

        if not first:
            work.append(functools.partial(column, 0))
            work.append(functools.partial(right, 0))
            work += [functools.partial(column, b) for b in range(1, m)]
            work += [functools.partial(right, a) for a in range(1, m)]
            work += [functools.partial(add_new, i, k - 1) for i in range(4)]
        total = len(work)
        at = [0]

        def hook():
            at[0] += 1
            if extra and at[0] in extra:
                do(*extra[at[0]])
            while work and total - len(work) < -(-total * at[0] // 15):
                work.pop(0)()

        W = join(inverse_factor(A[k, pl.ds(0, BLK), :].reshape(16, 8, BLK), hook))
        while work:
            work.pop(0)()
        if last:
            do(*last)
        here = rows(k * BLK, BLK)
        hi, lo = split(dot3_nn(W, split(B[here, :])))
        YH[...] = hi
        YL[...] = lo
        if m > 1:
            panel = join(dot3_nt(join(A[k, pl.ds(BLK, BLK * (m - 1)), :]), W))
            L[pl.ds(0, BLK * (m - 1)), :] = panel
            A[k + 1, pl.ds(0, BLK), :] -= dot3_nt(panel[:BLK], panel[:BLK])

    zp[...] = jnp.zeros(zp.shape, f32)
    zc[...] = jnp.zeros(zc.shape, f32)
    step(0, 8, first=True, extra={8: ("e2",)}, last=("f1", "g1"))
    step(1, 7, extra={8: ("f2",)}, last=("g2",))

    def six(k, carry):
        step(k, 6)
        return carry

    def three(k, carry):
        step(k, 3)
        return carry

    lax.fori_loop(2, 5, six, 0)
    lax.fori_loop(5, 8, three, 0)
    for i in range(4):
        add_new(i, NB - 1)

    columns = rows(me.g * BLK, BLK, BLK)

    def new_copy(p, to):
        return remote(zp.at[rows(to * UNIT, UNIT), :], out.at[:, columns], s_new.at[p], r_new.at[p], me.grp(to))

    each(lambda p: new_copy(p, lax.rem(me.g + p, 16)).start())
    out[:, columns] = zp[rows(me.g * UNIT, UNIT), :]

    new = zc[...]
    pair = dot3(nn, split(new.T * occ[...]), split(new))
    r = lax.broadcasted_iota(jnp.int32, (BLK, BLK), 0)
    c = lax.broadcasted_iota(jnp.int32, (BLK, BLK), 1)
    pair = jnp.where(r // 8 == c // 8, pair, 0.0)
    fold = jnp.where((lax.rem(r, 8) == lax.rem(c, 8)) & (c < UNIT), 1.0, 0.0).astype(bf16)
    hi, lo = split(pair)
    pair = jnp.where(lax.rem(r, 8) == c // 8, nn(hi, fold) + nn(lo, fold), 0.0)
    hi, lo = split(pair)
    atom = jnp.where(r[:8] == c[:8] // 8, 1.0, 0.0).astype(bf16)
    own_rho[...] = nn(atom, hi) + nn(atom, lo)
    mine = rows(me.d * 8, 8)

    def rho_copy(p, to):
        return remote(own_rho, all_rho.at[mine, :], s_rho.at[p], r_rho.at[p], me.dom(to))

    each(lambda p: rho_copy(p, lax.rem(me.d + p, 16)).start())
    all_rho[mine, :] = own_rho[...]
    weight = jnp.broadcast_to(occ[...] * (32768.0 / TOTAL), (8, TOTAL))
    dens[...] = dot3(nn, split(weight), split(zp[...] * zp[...]))[:1]

    def drain(p):
        psi_copy(p, me.g).wait_send()
        dom_copy(p, me.d).wait_send()
        cf_copy(p, me.g).wait_send()
        new_copy(p, me.g).wait()
        rho_copy(p, me.d).wait()

    each(drain)
    for copy in started:
        copy.wait_send()


def on_device(psi, proj, offsets, species, augment_q, rotation, occupation):
    states, cells = psi.shape
    channels = augment_q.shape[1]
    vm, sm, hbm = (pl.BlockSpec(memory_space=s) for s in (pltpu.VMEM, pltpu.SMEM, pl.ANY))
    dma, n = pltpu.SemaphoreType.DMA, len(CHUNK)
    sixteen = [dma((16,)), dma((16,))]
    new_psi, density, rho = pl.pallas_call(
        kernel,
        out_shape=(jax.ShapeDtypeStruct((states, cells), f32), jax.ShapeDtypeStruct((1, BLK), f32),
                   jax.ShapeDtypeStruct((BLK, BLK), f32)),
        in_specs=[hbm, hbm, sm, sm, vm, hbm, vm], out_specs=(vm, vm, vm),
        scratch_shapes=[
            pltpu.VMEM(psi.shape, f32), pltpu.VMEM(proj.shape, f32), pltpu.VMEM(rotation.shape, f32),
            pltpu.VMEM((2, TOTAL, TOTAL), bf16),
            pltpu.VMEM((16, 32, BLK), f32), pltpu.VMEM((16, 32, BLK), f32), pltpu.VMEM((16, 32, BLK), f32),
            pltpu.VMEM((TOTAL, BLK), f32), pltpu.VMEM((TOTAL, BLK), f32),
            pltpu.VMEM((TOTAL, 2 * BLK), bf16), pltpu.VMEM((TOTAL, 2 * BLK), bf16), pltpu.VMEM((NB, 2, UNIT, 2 * BLK), bf16),
            pltpu.VMEM((4, 8, BLK), f32),
            pltpu.VMEM((2, HALF, BLK), f32), pltpu.VMEM((HALF, BLK), f32), pltpu.VMEM((HALF, BLK), f32), pltpu.VMEM((HALF, BLK), f32),
            pltpu.VMEM((8, HALF // 8, BLK), f32), pltpu.VMEM((HALF // 8, BLK), f32),
            pltpu.VMEM((16, HALF // 8, BLK), f32), pltpu.VMEM((2, HALF, BLK), f32),
            pltpu.VMEM((PAD, TOTAL, BLK), f32), pltpu.VMEM((PAD * BLK, 2 * BLK), f32),
            pltpu.VMEM((TOTAL, 2 * BLK), bf16),
            pltpu.VMEM((BLK, 2 * BLK), bf16), pltpu.VMEM((BLK, 2 * BLK), bf16),
            pltpu.VMEM((TOTAL, BLK), f32), pltpu.VMEM((TOTAL, BLK), f32),
            pltpu.VMEM((8, BLK), f32),
            dma((3,)), *sixteen, *sixteen, *sixteen,
            dma((2 * n,)), dma((2 * n,)), dma((n, 2, 8)), dma((n, 2, 8)), dma((n, 2, 16)), dma((n, 2, 16)),
            *sixteen, *sixteen],
        compiler_params=pltpu.CompilerParams(collective_id=0, has_side_effects=True, vmem_limit_bytes=56 * 2**20),
    )(psi, proj, offsets, species, augment_q, rotation, occupation.reshape(1, TOTAL))
    return new_psi, density.reshape(BLK), rho[:, :channels * channels]


def solution(mesh):
    placed = (P("grp", "dom"), P("dom", None, None), P("dom"), P(), P(), P(), P())
    return jax.shard_map(
        on_device, mesh=mesh, in_specs=placed,
        out_specs=(P("grp", "dom"), P(("dom", "grp")), P()), check_vma=False)
```

time: 818 us -> 115 us (0.14); the launches traced: 806 us -> 115 us
  waiting for transfers between devices: 336 us -> 0 us
  other arithmetic: 261 us -> 0 us
  Pallas kernels: 0 us -> 109 us
  matrix products: 86.6 us -> 0 us
  blocking collectives: 61.4 us -> 0 us
  local copies, waits for them, and re-layouts: 38.9 us -> 4.58 us
  between operations: 21 us -> 1.29 us
    another operation x33 -> x0, other arithmetic: 256 us -> none  [the longest x30 172 us: on_device(): lower = jnp.linalg.cholesky(gram)]
    all_gather x3 -> x0, waiting for transfers between devices: 211 us -> none  [the longest x1 81.3 us: on_device(): lax.all_gather(psi, 'grp', axis=0, tiled=True)]
    psum x1 -> x0, waiting for transfers between devices: 125 us -> none  [on_device(): gram_rows_own = lax.psum(grid_part, 'dom') + paw_part]
    pallas_call x0 -> x1, Pallas kernels: none -> 109 us  [on_device(): pl.pallas_call(kernel, out_shape=(jax.ShapeDtypeStruct((states, cells), f...]
    unnamed x1 -> x0, blocking collectives: 61.4 us -> none
    another operation x29 -> x0, matrix products: 46 us -> none  [the longest x14 23.2 us: on_device(): lower = jnp.linalg.cholesky(gram)]
    dot_general x8 -> x0, matrix products: 40.6 us -> none  [the longest x5 38.4 us: product(): jnp.dot(left, right, precision=highest, preferred_element_type=jnp.float32)]
    another operation x37 -> x0, local copies, waits for them, and re-layouts: 25.7 us -> none
  transfers between devices with their start and end apart: 4 -> 0, of which waited for: 4 -> 0; matrix products, arithmetic and copies ran while one was open for 1% -> 0% of each run, Pallas kernels for 0% -> 0%
where the time goes in v2:
time: 115 us
  Pallas kernels  109 us (95%)
  local copies, waits for them, and re-layouts  4.58 us (4%)
  between operations  1.29 us (1%)
    pallas_call x1, Pallas kernels, on_device(): pl.pallas_call(kernel, out_shape=(jax.ShapeDtypeStruct((states, cells), f...  109 us
    unnamed x3, local copies, waits for them, and re-layouts  4.58 us

profile of v2, /device:TPU:1, one launch (start us, length us, event | category | flops | bytes accessed | tf_op | source)
XLA Modules:
  0.0 115.0 jit_solution(7648333998545105962)
XLA Ops:
  1.3 109.1 %shard_map.94 = (f32[64,2048]{1,0:T(8,128)}, f32[1,128]{1,0:T(1,128)}, f32[128,128]{1,0:T(8,128)}) custom-call(f32[64,2048]{1,0:T(8,128)} %psi.1, f32[1,128,2048]{2,1,0:T(8,128)} %proj.1, s32[1]{0:T(128)S(6)} %copy.13.off, s32[128]{0:T(128)} %species.1, f32[4,8,8]{2,1,0:T(8,128)} %aug.1, f32[1024,1024]{1,0:T(8,128)} %rot.1, f32[1,1024]{1,0:T(1,128)} %bitcast.4), custom_call_target="tpu_custom_call" | custom-call | tf_op jit(solution)/shard_map/pallas_call | solution.py:451
  110.4 1.5 %copy.10 = f32[128,64]{0,1:T(8,128)} copy(f32[128,64]{1,0:T(8,128)} %bitcast.3) | data formatting | bytes 65536
  112.0 1.9 %copy.14 = f32[64,2048]{1,0:T(8,128)} copy(f32[64,2048]{1,0:T(8,128)} %get-tuple-element.15) | data formatting | bytes 1048576
  113.8 1.2 %copy.15 = f32[128]{0:T(128)} copy(f32[128]{0:T(128)} %bitcast.5) | data formatting | bytes 1024

commit v3 on v2

--- a/solution.py
+++ b/solution.py
@@ -13,11 +13,12 @@
 TOTAL = NB * BLK
 UNIT = 64
 START = [sum(NB - j for j in range(c)) for c in range(NB + 1)]
-HALF = START[NB] * UNIT
-CHUNK = (4, 16, 16)
+CHUNK = (8, 8, 8, 8, 8)
+HALF = sum(CHUNK) * UNIT
 CH = [u * UNIT for u in CHUNK]
 CO = [sum(CH[:c]) for c in range(len(CH) + 1)]
-PAD = 10
+NEAR = 4
+PAD = 11
 
 
 def split(v):
@@ -58,6 +59,7 @@
     def __init__(self):
         self.d, self.g = lax.axis_index("dom"), lax.axis_index("grp")
         self.core, self.chip = lax.rem(self.g, 2), self.g // 2
+        self.z, self.ylo = self.d // 2, lax.rem(self.d, 2)
 
     def dom(self, i):
         return {"dom": i, "grp": self.g}
@@ -78,7 +80,7 @@
         return carry
 
     lax.fori_loop(1, 16, one, 0)
-    pl.semaphore_wait(barrier, 30)
+    return lambda: pl.semaphore_wait(barrier, 30)
 
 
 def remote(src, dst, send, recv, device):
@@ -91,32 +93,34 @@
 
 
 def recip(a):
-    r = pl.reciprocal(a, approx=True)
-    return r * (2.0 - a * r)
+    return pltpu.reciprocal(a, approx=True)
 
 
 def inverse_factor(V, hook):
     row = lax.broadcasted_iota(jnp.int32, (8, BLK), 0)
-    where = lax.broadcasted_iota(jnp.int32, (16, 8, BLK), 0) * 8 + lax.broadcasted_iota(jnp.int32, (16, 8, BLK), 1)
-    W = jnp.where(lax.broadcasted_iota(jnp.int32, (16, 8, BLK), 2) == where, 1.0, 0.0).astype(f32)
+    lane = lax.broadcasted_iota(jnp.int32, (8, BLK), 1)
     out = []
     for j in range(16):
-        col = [jnp.broadcast_to(V[:, :, 8 * j + t:8 * j + t + 1], V.shape) for t in range(8)]
+        n = min(NEAR, 15 - j)
+        col = [jnp.broadcast_to(V[:n + 1, :, 8 * j + t:8 * j + t + 1], (n + 1, 8, BLK)) for t in range(8)]
         D = {(s, t): row_b(col[t][0], s) for t in range(8) for s in range(t, 8)}
-        RA = [row_b(V[0], t) for t in range(8)]
-        RW = [row_b(W[0], t) for t in range(8)]
+        here = lane // 8 == j
+        first = jnp.where(here, jnp.where(lane == row + 8 * j, 1.0, 0.0), V[0])
+        R = [row_b(first, t) for t in range(8)]
+        if n:
+            C = [c[1:] for c in col]
+            V = jnp.where(here[None], 0.0, V[1:])
+            N, F = V[:n], V[n:]
         scale = []
-        more = j < 15
-        if more:
-            C = [c[1:] for c in col]
-            V, W = V[1:], W[1:]
+        f = [recip(D[t, t]) for t in range(1, 8, 2)]
         for t0 in range(0, 8, 2):
             t1 = t0 + 1
             a, b, c = D[t0, t0], D[t1, t0], D[t1, t1]
-            det = a * c - b * b
+            size = f[t0 // 2]
+            det = a * (c * size) - b * (b * size)
             r0 = recip(a)
-            r1 = a * recip(det)
-            D[t1, t1] = det * r0
+            r1 = (a * size) * recip(det)
+            D[t1, t1] = c - (b * r0) * b
             scale += [lax.rsqrt(a), lax.rsqrt(D[t1, t1])]
             for t, r in ((t0, r0), (t1, r1)):
                 l = {s: D[s, t] * r for s in range(t + 1, 8)}
@@ -125,32 +129,39 @@
                         if not (s == t1 and t == t0):
                             D[s, u] = D[s, u] - l[s] * D[u, t]
                 for s in range(t + 1, 8):
-                    RA[s] = RA[s] - l[s] * RA[t]
-                    RW[s] = RW[s] - l[s] * RW[t]
-                if more:
+                    R[s] = R[s] - l[s] * R[t]
+                if n:
                     li = C[t] * r[None]
                     for u in range(t + 1, 8):
                         C[u] = C[u] - li * D[u, t][None]
-                    V = V - li * RA[t][None]
-                    W = W - li * RW[t][None]
-        w = RW[0] * scale[0]
+                    N = N - li * R[t][None]
+        w = R[0] * scale[0]
         for t in range(1, 8):
-            w = jnp.where(row == t, RW[t] * scale[t], w)
-        out.append(w)
+            w = jnp.where(row == t, R[t] * scale[t], w)
+        out.append(jnp.where(lane < 8 * j + 8, w, 0.0))
+        if n < 15 - j:
+            hi = w.astype(bf16).astype(f32)
+            lo = w - hi
+            left = jnp.concatenate([hi, hi, lo], axis=0).T[8 * (j + 1 + n):].astype(bf16)
+            right = jnp.concatenate([hi, lo, hi], axis=0).astype(bf16)
+            F = F - nn(left, right).reshape(15 - j - n, 8, BLK)
+            V = jnp.concatenate([N, F], axis=0)
+        elif n:
+            V = N
         hook()
     return jnp.concatenate(out, axis=0)
 
 
 def kernel(psi, proj, off, species, aug, rot, occ, out, dens, all_rho,
-           psi_v, proj_v, rot_v, rt, placed, got, cp, pc, cf, ps, cs, ws, tiled, t, tp, rc, h, r1, q1, r2, o,
-           A, B, L, YH, YL, zp, zc, own_rho,
-           s_in, s_psi, r_psi, s_dom, r_dom, s_cf, r_cf, s_core, r_core, s_x, r_x, s_z, r_z, s_new, r_new, s_rho, r_rho):
+           psi_v, proj_v, rot_v, rt, placed, got, cp, pc, cf, ps, cs, ws, tiled, t, tp, rc, h, r1, q1, r2, q2, r3, o,
+           A, B, L, WJ, YH, YL, zp, zc, own_rho,
+           s_in, s_psi, r_psi, s_dom, r_dom, s_cf, r_cf, s_core, r_core, s_x, r_x, s_z, r_z, s_y, r_y, s_new, r_new, s_rho, r_rho):
     me = Place()
     loads = [pltpu.make_async_copy(src, dst, s_in.at[i])
              for i, (src, dst) in enumerate(((psi, psi_v), (proj, proj_v), (rot, rot_v)))]
     for load in loads:
         load.start()
-    greet(me)
+    met = greet(me)
     own = rows(me.g * UNIT, UNIT)
 
     def psi_copy(p, to):
@@ -167,8 +178,6 @@
             body(p)
             return carry
         lax.fori_loop(1, 16, one, 0)
-
-    each(lambda p: psi_copy(p, lax.rem(me.g + p, 16)).start())
 
     loads[0].wait()
     loads[1].wait()
@@ -181,7 +190,9 @@
     for d in range(16):
         pick = jnp.where(gap == UNIT * d, 1.0, 0.0).astype(bf16)
         placed[d] = nn(value[0], pick) + nn(value[1], pick)
+    met()
     each(lambda p: dom_copy(p, lax.rem(me.d + p, 16)).start())
+    each(lambda p: psi_copy(p, lax.rem(me.g + p, 16)).start())
 
     A[...] = jnp.zeros(A.shape, f32)
     B[pl.ds(TOTAL, (PAD - NB) * BLK), :] = jnp.zeros(((PAD - NB) * BLK, 2 * BLK), f32)
@@ -227,8 +238,8 @@
     def chips(c, i, source, target):
         return spread(8, me.chip, lambda to: me.grp(to * 2 + me.core), source, target, s_x.at[c, i], r_x.at[c, i])
 
-    def doms(c, i, source, target):
-        return spread(16, me.d, me.dom, source, target, s_z.at[c, i], r_z.at[c, i])
+    def along_z(c, i, source, target):
+        return spread(8, me.z, lambda to: me.dom(to * 2 + me.ylo), source, target, s_z.at[c, i], r_z.at[c, i])
 
     def sizes(c):
         return CO[c], CH[c], CO[c] // 8, CH[c] // 8
@@ -252,45 +263,44 @@
         total = r1[0, part]
         for i in range(1, 8):
             total = total + r1[i, part]
-        if c == 0:
-            r2[me.d, part] = total
-            waits["c", c] = doms(c, 0, lambda to: r2.at[me.d, part], r2.at[me.d, part])
-        else:
-            q1[part] = total
-            m = n // 16
-            waits["c", c] = doms(c, 0, lambda to: q1.at[rows(at + to * m, m)], r2.at[me.d, pl.ds(at, m)])
+        q1[part] = total
+        m = n // 8
+        waits["c", c] = along_z(c, 0, lambda to: q1.at[rows(at + to * m, m)], r2.at[me.z, pl.ds(at, m)])
 
     def step_d(c):
         arrive(("c", c))
         first, count, at, n = sizes(c)
-        if c == 0:
-            part, here = pl.ds(at, n), o.at[me.core, rows(first + me.chip * n, n)]
-        else:
-            m = n // 16
-            part, here = pl.ds(at, m), o.at[me.core, rows(first + me.chip * n + me.d * m, m)]
-            r2[me.d, part] = q1[rows(at + me.d * m, m)]
+        m = n // 8
+        part = pl.ds(at, m)
+        r2[me.z, part] = q1[rows(at + me.z * m, m)]
         total = r2[0, part]
-        for i in range(1, 16):
+        for i in range(1, 8):
             total = total + r2[i, part]
-        here[...] = total
-        if c:
-            waits["d", c] = doms(c, 1, lambda to: here, here)
+        q2[part] = total
+        waits["d", c] = [go(remote(q2.at[part], r3.at[part], s_y.at[c], r_y.at[c], me.dom(me.d + 1 - 2 * me.ylo)))]
 
     def step_e(c):
-        if c:
-            arrive(("d", c))
+        arrive(("d", c))
+        first, count, at, n = sizes(c)
+        m = n // 8
+        here = o.at[me.core, rows(first + me.chip * n + me.z * m, m)]
+        here[...] = q2[pl.ds(at, m)] + r3[pl.ds(at, m)]
+        waits["e", c] = along_z(c, 1, lambda to: here, here)
+
+    def step_f(c):
+        arrive(("e", c))
         first, count, at, n = sizes(c)
         here = o.at[me.core, rows(first + me.chip * n, n)]
-        waits["e", c] = chips(c, 1, lambda to: here, here)
-
-    def step_f(c):
-        arrive(("e", c))
+        waits["f", c] = chips(c, 1, lambda to: here, here)
+
+    def step_g(c):
+        arrive(("f", c))
         here = o.at[me.core, pl.ds(CO[c], CH[c])]
         n = len(CHUNK) + c
-        waits["f", c] = [go(remote(here, here, s_core.at[n], r_core.at[n], me.other_core()))]
-
-    def step_g(c):
-        arrive(("f", c))
+        waits["g", c] = [go(remote(here, here, s_core.at[n], r_core.at[n], me.other_core()))]
+
+    def step_h(c):
+        arrive(("g", c))
         for col in range(NB):
             for r in range(NB - col):
                 unit = START[col] + r
@@ -300,16 +310,19 @@
 
     def do(*names):
         for name in names:
-            {"a": step_a, "b": step_b, "c": step_c, "d": step_d, "e": step_e, "f": step_f, "g": step_g}[name[0]](int(name[1]))
+            {"a": step_a, "b": step_b, "c": step_c, "d": step_d, "e": step_e, "f": step_f, "g": step_g, "h": step_h}[name[0]](int(name[1]))
 
     def gram_of_psi():
         ready = 0
+        padding = pl.ds(START[NB] * UNIT, HALF - START[NB] * UNIT)
+        t[:, padding] = jnp.zeros((2, HALF - START[NB] * UNIT, BLK), f32)
+        tp[padding] = jnp.zeros((HALF - START[NB] * UNIT, BLK), f32)
         for c in range(NB):
             part = dot3_nt(ps[BLK * c:], ps[BLK * c:BLK * c + BLK])
             for r in range(NB - c):
                 for half in range(2):
                     t[half, pl.ds(UNIT * (START[c] + r), UNIT)] = part[BLK * r + UNIT * half: BLK * r + UNIT * half + UNIT]
-            while ready < len(CHUNK) and CO[ready + 1] <= START[c + 1] * UNIT:
+            while ready < len(CHUNK) and (CO[ready + 1] <= START[c + 1] * UNIT or c == NB - 1):
                 step_a(ready)
                 ready += 1
 
@@ -319,7 +332,7 @@
     each(lambda p: psi_copy(p, me.g).wait_recv())
     ps[...] = join(pc[...])
     gram_of_psi()
-    do("b0", "b1")
+    do("b0", "b1", "b2", "b3", "b4")
     B[:TOTAL, :BLK] = pc[...]
 
     each(lambda p: cf_copy(p, me.g).wait_recv())
@@ -332,9 +345,9 @@
     for c in range(NB):
         own_rows = ws[c:, me.core].reshape((NB - c) * UNIT, 2 * BLK)
         tp[pl.ds(START[c] * UNIT, (NB - c) * UNIT)] = dot3_nt(own_rows, cs[BLK * c:BLK * c + BLK])
-    do("c0", "b2")
+    do("c0", "c1")
     B[:TOTAL, BLK:] = cf[...]
-    do("c1", "d0", "e0", "c2", "d1", "f0", "d2", "e1", "g0")
+    do("c2", "d0", "c3", "d1", "e0", "e1", "d2", "c4", "e2", "f0", "d3", "f1", "e3", "d4", "f2", "g0", "h0")
 
     def add_new(i, k):
         piece, past = pl.ds(2 * BLK * i, 2 * BLK), rows(k * BLK, BLK, BLK)
@@ -342,11 +355,23 @@
         zp[piece] += new[:, :BLK]
         zc[piece] += new[:, BLK:]
 
+    def finish(k, m):
+        def panel(a, n):
+            past = A[k, pl.ds(BLK * (a + 1), BLK * n), :]
+            L[pl.ds(BLK * a, BLK * n), :] = join(dot3_nt(join(past), WJ[...]))
+
+        def substitute():
+            hi, lo = split(dot3_nn(WJ[...], split(B[rows(k * BLK, BLK), :])))
+            YH[...] = hi
+            YL[...] = lo
+
+        return [functools.partial(panel, a, min(2, m - a)) for a in range(1, m, 2)], substitute
+
     def step(k, m, first=False, extra=None, last=()):
         work = []
 
         def column(b):
-            n = max(m - b, 0) if b else m - 1
+            n = m - b if b else m - 1
             a = b if b else 1
             A[k + b, pl.ds(BLK * (a - b), BLK * n), :] -= dot3_nt(L[pl.ds(BLK * a, BLK * n), :], L[pl.ds(BLK * b, BLK), :])
 
@@ -354,7 +379,10 @@
             B[rows((k + a) * BLK, BLK), :] -= dot3_nn(L[pl.ds(BLK * a, BLK), :], (YH[...], YL[...]))
 
         if not first:
+            panels, substitute = finish(k - 1, m)
+            work += panels
             work.append(functools.partial(column, 0))
+            work.append(substitute)
             work.append(functools.partial(right, 0))
             work += [functools.partial(column, b) for b in range(1, m)]
             work += [functools.partial(right, a) for a in range(1, m)]
@@ -372,32 +400,26 @@
         W = join(inverse_factor(A[k, pl.ds(0, BLK), :].reshape(16, 8, BLK), hook))
         while work:
             work.pop(0)()
-        if last:
-            do(*last)
-        here = rows(k * BLK, BLK)
-        hi, lo = split(dot3_nn(W, split(B[here, :])))
-        YH[...] = hi
-        YL[...] = lo
+        WJ[...] = W
         if m > 1:
-            panel = join(dot3_nt(join(A[k, pl.ds(BLK, BLK * (m - 1)), :]), W))
-            L[pl.ds(0, BLK * (m - 1)), :] = panel
-            A[k + 1, pl.ds(0, BLK), :] -= dot3_nt(panel[:BLK], panel[:BLK])
+            top = join(dot3_nt(join(A[k, pl.ds(BLK, BLK), :]), W))
+            L[pl.ds(0, BLK), :] = top
+            A[k + 1, pl.ds(0, BLK), :] -= dot3_nt(top, top)
+        do(*last)
 
     zp[...] = jnp.zeros(zp.shape, f32)
     zc[...] = jnp.zeros(zc.shape, f32)
-    step(0, 8, first=True, extra={8: ("e2",)}, last=("f1", "g1"))
-    step(1, 7, extra={8: ("f2",)}, last=("g2",))
-
-    def six(k, carry):
-        step(k, 6)
+    step(0, 8, first=True, extra={1: ("e4",), 5: ("f3",), 10: ("g1",)}, last=("h1",))
+    step(1, 7, extra={2: ("f4",), 6: ("g2",)}, last=("h2",))
+    step(2, 6, extra={4: ("g3",)}, last=("h3",))
+    step(3, 5, extra={4: ("g4",)}, last=("h4",))
+
+    def four(k, carry):
+        step(k, 4)
         return carry
 
-    def three(k, carry):
-        step(k, 3)
-        return carry
-
-    lax.fori_loop(2, 5, six, 0)
-    lax.fori_loop(5, 8, three, 0)
+    lax.fori_loop(4, 8, four, 0)
+    finish(NB - 1, 1)[1]()
     for i in range(4):
         add_new(i, NB - 1)
 
@@ -462,14 +484,15 @@
             pltpu.VMEM((4, 8, BLK), f32),
             pltpu.VMEM((2, HALF, BLK), f32), pltpu.VMEM((HALF, BLK), f32), pltpu.VMEM((HALF, BLK), f32), pltpu.VMEM((HALF, BLK), f32),
             pltpu.VMEM((8, HALF // 8, BLK), f32), pltpu.VMEM((HALF // 8, BLK), f32),
-            pltpu.VMEM((16, HALF // 8, BLK), f32), pltpu.VMEM((2, HALF, BLK), f32),
+            pltpu.VMEM((8, HALF // 8, BLK), f32), pltpu.VMEM((HALF // 8, BLK), f32), pltpu.VMEM((HALF // 8, BLK), f32),
+            pltpu.VMEM((2, HALF, BLK), f32),
             pltpu.VMEM((PAD, TOTAL, BLK), f32), pltpu.VMEM((PAD * BLK, 2 * BLK), f32),
-            pltpu.VMEM((TOTAL, 2 * BLK), bf16),
+            pltpu.VMEM((TOTAL, 2 * BLK), bf16), pltpu.VMEM((BLK, 2 * BLK), bf16),
             pltpu.VMEM((BLK, 2 * BLK), bf16), pltpu.VMEM((BLK, 2 * BLK), bf16),
             pltpu.VMEM((TOTAL, BLK), f32), pltpu.VMEM((TOTAL, BLK), f32),
             pltpu.VMEM((8, BLK), f32),
             dma((3,)), *sixteen, *sixteen, *sixteen,
-            dma((2 * n,)), dma((2 * n,)), dma((n, 2, 8)), dma((n, 2, 8)), dma((n, 2, 16)), dma((n, 2, 16)),
+            dma((2 * n,)), dma((2 * n,)), dma((n, 2, 8)), dma((n, 2, 8)), dma((n, 2, 8)), dma((n, 2, 8)), dma((n,)), dma((n,)),
             *sixteen, *sixteen],
         compiler_params=pltpu.CompilerParams(collective_id=0, has_side_effects=True, vmem_limit_bytes=56 * 2**20),
     )(psi, proj, offsets, species, augment_q, rotation, occupation.reshape(1, TOTAL))

time: 115 us -> 108 us (0.939)
  Pallas kernels: 109 us -> 102 us
    pallas_call x1, Pallas kernels: 109 us -> 102 us  [on_device(): pl.pallas_call(kernel, out_shape=(jax.ShapeDtypeStruct((states, cells), f...]
where the time goes in v3:
time: 108 us
  Pallas kernels  102 us (94%)
  local copies, waits for them, and re-layouts  4.58 us (4%)
  between operations  1.29 us (1%)
    pallas_call x1, Pallas kernels, on_device(): pl.pallas_call(kernel, out_shape=(jax.ShapeDtypeStruct((states, cells), f...  102 us
    unnamed x3, local copies, waits for them, and re-layouts  4.58 us

profile of v3, /device:TPU:1, one launch (start us, length us, event | category | flops | bytes accessed | tf_op | source)
XLA Modules:
  0.0 108.1 jit_solution(1285437683151458582)
XLA Ops:
  1.3 102.2 %shard_map.94 = (f32[64,2048]{1,0:T(8,128)}, f32[1,128]{1,0:T(1,128)}, f32[128,128]{1,0:T(8,128)}) custom-call(f32[64,2048]{1,0:T(8,128)} %psi.1, f32[1,128,2048]{2,1,0:T(8,128)} %proj.1, s32[1]{0:T(128)S(6)} %copy.13.off, s32[128]{0:T(128)} %species.1, f32[4,8,8]{2,1,0:T(8,128)} %aug.1, f32[1024,1024]{1,0:T(8,128)} %rot.1, f32[1,1024]{1,0:T(1,128)} %bitcast.4), custom_call_target="tpu_custom_call" | custom-call | tf_op jit(solution)/shard_map/pallas_call | solution.py:473
  103.5 1.5 %copy.10 = f32[128,64]{0,1:T(8,128)} copy(f32[128,64]{1,0:T(8,128)} %bitcast.3) | data formatting | bytes 65536
  105.0 1.9 %copy.14 = f32[64,2048]{1,0:T(8,128)} copy(f32[64,2048]{1,0:T(8,128)} %get-tuple-element.15) | data formatting | bytes 1048576
  106.9 1.2 %copy.15 = f32[128]{0:T(128)} copy(f32[128]{0:T(128)} %bitcast.5) | data formatting | bytes 1024

commit v4 on v3

--- a/solution.py
+++ b/solution.py
@@ -195,6 +195,8 @@
     each(lambda p: psi_copy(p, lax.rem(me.g + p, 16)).start())
 
     A[...] = jnp.zeros(A.shape, f32)
+    zp[...] = jnp.zeros(zp.shape, f32)
+    zc[...] = jnp.zeros(zc.shape, f32)
     B[pl.ds(TOTAL, (PAD - NB) * BLK), :] = jnp.zeros(((PAD - NB) * BLK, 2 * BLK), f32)
     lane = lax.broadcasted_iota(jnp.int32, (8, BLK), 1)
     repeat = jnp.where(lax.broadcasted_iota(jnp.int32, (8, BLK), 0) == lax.rem(lane, 8), 1.0, 0.0)
@@ -345,7 +347,9 @@
     for c in range(NB):
         own_rows = ws[c:, me.core].reshape((NB - c) * UNIT, 2 * BLK)
         tp[pl.ds(START[c] * UNIT, (NB - c) * UNIT)] = dot3_nt(own_rows, cs[BLK * c:BLK * c + BLK])
-    do("c0", "c1")
+        if c == 0:
+            do("c0")
+    do("c1")
     B[:TOTAL, BLK:] = cf[...]
     do("c2", "d0", "c3", "d1", "e0", "e1", "d2", "c4", "e2", "f0", "d3", "f1", "e3", "d4", "f2", "g0", "h0")
 
@@ -407,8 +411,6 @@
             A[k + 1, pl.ds(0, BLK), :] -= dot3_nt(top, top)
         do(*last)
 
-    zp[...] = jnp.zeros(zp.shape, f32)
-    zc[...] = jnp.zeros(zc.shape, f32)
     step(0, 8, first=True, extra={1: ("e4",), 5: ("f3",), 10: ("g1",)}, last=("h1",))
     step(1, 7, extra={2: ("f4",), 6: ("g2",)}, last=("h2",))
     step(2, 6, extra={4: ("g3",)}, last=("h3",))
@@ -420,15 +422,18 @@
 
     lax.fori_loop(4, 8, four, 0)
     finish(NB - 1, 1)[1]()
+    columns = rows(me.g * BLK, BLK, BLK)
+
+    def new_copy(p, to):
+        return remote(zp.at[rows(to * UNIT, UNIT), :], out.at[:, columns], s_new.at[p], r_new.at[p], me.grp(to))
+
     for i in range(4):
         add_new(i, NB - 1)
-
-    columns = rows(me.g * BLK, BLK, BLK)
-
-    def new_copy(p, to):
-        return remote(zp.at[rows(to * UNIT, UNIT), :], out.at[:, columns], s_new.at[p], r_new.at[p], me.grp(to))
-
-    each(lambda p: new_copy(p, lax.rem(me.g + p, 16)).start())
+        for to in range(4 * i, 4 * i + 4):
+            @pl.when(me.g != to)
+            def _():
+                new_copy(lax.rem(to - me.g + 16, 16), to).start()
+
     out[:, columns] = zp[rows(me.g * UNIT, UNIT), :]
 
     new = zc[...]

time: 108 us -> 108 us (level)
  no operation moved by 1% of the time
where the time goes in v4:
time: 108 us
  Pallas kernels  102 us (94%)
  local copies, waits for them, and re-layouts  4.58 us (4%)
  between operations  1.29 us (1%)
    pallas_call x1, Pallas kernels, on_device(): pl.pallas_call(kernel, out_shape=(jax.ShapeDtypeStruct((states, cells), f...  102 us
    unnamed x3, local copies, waits for them, and re-layouts  4.58 us

profile of v4, /device:TPU:1, one launch (start us, length us, event | category | flops | bytes accessed | tf_op | source)
XLA Modules:
  0.0 107.8 jit_solution(8499079384666070960)
XLA Ops:
  1.3 101.9 %shard_map.94 = (f32[64,2048]{1,0:T(8,128)}, f32[1,128]{1,0:T(1,128)}, f32[128,128]{1,0:T(8,128)}) custom-call(f32[64,2048]{1,0:T(8,128)} %psi.1, f32[1,128,2048]{2,1,0:T(8,128)} %proj.1, s32[1]{0:T(128)S(6)} %copy.13.off, s32[128]{0:T(128)} %species.1, f32[4,8,8]{2,1,0:T(8,128)} %aug.1, f32[1024,1024]{1,0:T(8,128)} %rot.1, f32[1,1024]{1,0:T(1,128)} %bitcast.4), custom_call_target="tpu_custom_call" | custom-call | tf_op jit(solution)/shard_map/pallas_call | solution.py:478
  103.2 1.5 %copy.10 = f32[128,64]{0,1:T(8,128)} copy(f32[128,64]{1,0:T(8,128)} %bitcast.3) | data formatting | bytes 65536
  104.7 1.9 %copy.14 = f32[64,2048]{1,0:T(8,128)} copy(f32[64,2048]{1,0:T(8,128)} %get-tuple-element.15) | data formatting | bytes 1048576
  106.6 1.2 %copy.15 = f32[128]{0:T(128)} copy(f32[128]{0:T(128)} %bitcast.5) | data formatting | bytes 1024
